TPU v7x, 32 devices: a whole 2x2x4 slice. The times are simulated.
32 devices in a mesh: grp: 2 (over y), tm: 8 (over z, x), space: 2 (over core).
Axes of the slice: x: 2, y: 2, z: 4, core: 2. Of those that a mesh axis runs over, the one named last changes fastest.
Arguments:
- tokens: bfloat16 [16, 24, 64, 1024], P(('grp', 'tm'), 'space'), parts along dimension 0, may hold values from -28 to 28
- gains: float32 [2, 1024], replicated, may hold values from 0.5 to 2
- qkv_weights: bfloat16 [2, 1024, 1536], replicated, may hold values from -1.125 to 1.125
- out_weights: bfloat16 [2, 512, 1024], replicated, may hold values from -0.25 to 0.25
Outputs:
- video_out: bfloat16 [16, 24, 64, 1024], P(('grp', 'tm'), 'space'), parts along dimension 0
There are 2 independent parts, one for each index of `grp`. A program takes and returns all parts, laid end to end along the dimension named above; an argument that names none is the same for every part. Nothing has to cross between parts.
All inputs are finite; a program needn't handle non-finite values.
Results may differ from a plain program's by a relative error of at most 0.007.
Values may be sent and summed in bfloat16 or wider, within the bound.
A program may use at most 64 MiB of HBM per device.

v0:
```python
import jax
import jax.numpy as jnp
from jax import lax
from jax.sharding import PartitionSpec as P

HEADS = 8
HEAD = 64


def block_groups(groups, length):
    target = max(1, 512 // length)
    chosen = 1
    for candidate in range(1, min(groups, target) + 1):
        if groups % candidate == 0:
            chosen = candidate
    return chosen


def attend(tokens, length, gain_row, qkv_weight, out_weight):
    tok_count, feat_count = tokens.shape
    inner_width = out_weight.shape[0]
    stream = tokens.astype(jnp.float32)
    normed = (
        stream * lax.rsqrt(jnp.mean(stream * stream, axis=-1, keepdims=True) + 1e-06) * gain_row
    ).astype(jnp.bfloat16)
    projected = jnp.dot(normed, qkv_weight, preferred_element_type=jnp.float32).astype(jnp.bfloat16)
    per_block = block_groups(tok_count // length, length) * length
    blocks = tok_count // per_block
    shaped = projected.reshape(blocks, per_block, 3, HEADS, HEAD)
    scores = jnp.einsum(
        "bqhd,bkhd->bhqk", shaped[:, :, 0], shaped[:, :, 1], preferred_element_type=jnp.float32
    ) * HEAD ** (-0.5)
    group_ids = jnp.arange(per_block) // length
    same_group = group_ids[:, None] == group_ids[None, :]
    scores = jnp.where(same_group, scores, -1e30)
    row_max = jnp.max(scores, axis=-1, keepdims=True)
    raised = jnp.exp(scores - row_max)
    weights = (raised / jnp.sum(raised, axis=-1, keepdims=True)).astype(jnp.bfloat16)
    mixture = jnp.einsum(
        "bhqk,bkhd->bqhd", weights, shaped[:, :, 2], preferred_element_type=jnp.float32
    ).astype(jnp.bfloat16)
    mixture = mixture.reshape(tok_count, inner_width)
    update = jnp.dot(mixture, out_weight, preferred_element_type=jnp.float32)
    return (stream + update).astype(jnp.bfloat16)


def shards(tokens, gains, qkv_weights, out_weights):
    spread = lax.axis_size("space")
    frame_count = lax.axis_size("tm")
    frame_tokens = tokens[0]
    row_count, col_count, feat_count = frame_tokens.shape
    half_cols = col_count // spread
    transposed = jnp.transpose(frame_tokens, (1, 0, 2)).reshape(
        spread, half_cols, row_count, feat_count
    )
    piece = lax.all_to_all(transposed, "space", split_axis=0, concat_axis=2, tiled=True)
    col_items = piece.shape[1]
    height_n = piece.shape[2]
    flat = piece.reshape(col_items * height_n, feat_count)
    done = attend(flat, height_n, gains[0], qkv_weights[0], out_weights[0])
    columns_done = done.reshape(1, col_items, height_n, feat_count)
    regrouped = columns_done.reshape(half_cols, spread, row_count, feat_count).transpose(0, 2, 1, 3)
    span = col_count * row_count // frame_count
    regrouped = regrouped.reshape(frame_count, span, 1, feat_count)
    piece = lax.all_to_all(regrouped, "tm", split_axis=0, concat_axis=2, tiled=True)
    pos_items = piece.shape[1]
    frame_n = piece.shape[2]
    flat = piece.reshape(pos_items * frame_n, feat_count)
    done = attend(flat, frame_n, gains[1], qkv_weights[1], out_weights[1])
    timed = done.reshape(1, pos_items, frame_n, feat_count)
    paired = timed.reshape(span // spread, spread, frame_count, feat_count).transpose(0, 2, 1, 3)
    paired = paired.reshape(span // spread, frame_count * spread, feat_count)
    back_rows = lax.all_to_all(paired, ("tm", "space"), split_axis=1, concat_axis=0, tiled=True)
    back_rows = back_rows.reshape(frame_count, spread, span // spread, feat_count).transpose(
        1, 0, 2, 3
    )
    restored = back_rows.reshape(col_count, row_count, feat_count)
    return jnp.transpose(restored, (1, 0, 2))[None]


def solution(mesh):
    return jax.shard_map(
        shards,
        mesh=mesh,
        in_specs=(P(("grp", "tm"), "space", None, None), P(), P(), P()),
        out_specs=P(("grp", "tm"), "space", None, None),
        check_vma=False,
    )
```

profile of v0, /device:TPU:0, one launch (start us, length us, event | category | flops | bytes accessed | tf_op | source)
XLA Modules:
  0.0 206.8 jit_solution(540313732590014101)
XLA Ops:
  0.0 2.7 %copy.114 = bf16[2,32,12,1024]{3,1,2,0:T(8,128)(2,1)} copy(bf16[2,32,12,1024]{3,1,0,2:T(8,128)(2,1)} %bitcast.161) | data formatting | bytes 3145728 | tf_op jit(solution)/shard_map/reshape | solution.py:53
  2.7 3.8 %all-to-all-start = ((bf16[2,32,12,1024]{3,1,2,0:T(8,128)(2,1)}), bf16[2,32,12,1024]{3,1,2,0:T(8,128)(2,1)S(1)}, u32[]{:S(2)}, u32[]{:S(2)}) async-start(bf16[2,32,12,1024]{3,1,2,0:T(8,128)(2,1)} %copy.114), calls=%async_computation | async-start | bytes 3145728 | tf_op jit(solution)/shard_map/all_to_all | solution.py:56
  6.6 2.5 %all-to-all-done = bf16[2,32,12,1024]{3,1,2,0:T(8,128)(2,1)S(1)} async-done(((bf16[2,32,12,1024]{3,1,2,0:T(8,128)(2,1)}), bf16[2,32,12,1024]{3,1,2,0:T(8,128)(2,1)S(1)}, u32[]{:S(2)}, u32[]{:S(2)}) %all-to-all-start) | async-done | bytes 1572896 | tf_op jit(solution)/shard_map/all_to_all | solution.py:56
  9.9 2.2 %copy.116 = bf16[1,32,2,12,1024]{4,3,2,1,0:T(8,128)(2,1)} copy(bf16[1,32,2,12,1024]{4,1,3,2,0:T(8,128)(2,1)S(1)} %multiply_convert_fusion) | data formatting | bytes 3145728 | tf_op jit(solution)/shard_map/convert_element_type | solution.py:25
  12.1 2.5 %convert_element_type.84 = bf16[768,1024]{1,0:T(8,128)(2,1)S(1)} reshape(bf16[1,32,2,12,1024]{4,3,2,1,0:T(8,128)(2,1)} %copy.116) | data formatting | bytes 3145728 | tf_op jit(solution)/shard_map/convert_element_type | solution.py:25
  14.6 5.7 %convolution_convert_fusion.1 = bf16[768,1536]{1,0:T(8,128)(2,1)} fusion(bf16[768,1024]{1,0:T(8,128)(2,1)S(1)} %convert_element_type.84, bf16[2,1024,1536]{2,1,0:T(8,128)(2,1)} %param.6), kind=kOutput, calls=%fused_computation.23 | convolution fusion | flops 2417098752 | bytes 7077888 | tf_op jit(solution)/shard_map/dot_general | solution.py:26
  20.3 6.9 %reshape.162 = bf16[2,384,3,8,64]{4,3,2,1,0:T(8,128)(2,1)} reshape(bf16[768,1536]{1,0:T(8,128)(2,1)} %convolution_convert_fusion.1) | data formatting | bytes 4718592 | tf_op jit(solution)/shard_map/reshape | solution.py:29
  27.3 4.3 %fusion.75 = (bf16[2,384,1,8,64]{4,3,2,1,0:T(8,128)(2,1)S(1)}, bf16[2,384,1,8,64]{4,3,2,1,0:T(8,128)(2,1)}, bf16[2,384,1,8,64]{4,3,2,1,0:T(8,128)(2,1)}) fusion(bf16[2,384,3,8,64]{4,3,2,1,0:T(8,128)(2,1)} %reshape.162), kind=kLoop, calls=%fused_computation.86 | loop fusion | bytes 4718592 | tf_op jit(solution)/shard_map/slice | solution.py:40
  31.6 2.7 %copy.144 = bf16[2,384,1,8,64]{1,4,3,0,2:T(8,128)(2,1)} copy(bf16[2,384,1,8,64]{4,3,2,1,0:T(8,128)(2,1)} %get-tuple-element.9) | data formatting | bytes 1572864
  34.3 2.7 %copy.145 = bf16[2,384,1,8,64]{1,4,3,0,2:T(8,128)(2,1)} copy(bf16[2,384,1,8,64]{4,3,2,1,0:T(8,128)(2,1)} %get-tuple-element.10) | data formatting | bytes 1572864
  37.2 1.7 copy.143
  38.9 8.2 %fusion.77 = (f32[2,8,384]{2,1,0:T(8,128)S(1)}, f32[2,8,384,384]{2,3,1,0:T(8,128)}) fusion(pred[384,384]{0,1:T(8,128)(4,1)S(1)} %broadcast_compare_fusion.1, bf16[2,384,1,8,64]{1,4,3,0,2:T(8,128)(2,1)} %copy.145, bf16[2,384,1,8,64]{1,4,3,0,2:T(8,128)(2,1)} %copy.144), kind=kOutput, calls=%fused_computation.88 | convolution fusion | flops 311427456 | bytes 11182080 | tf_op jit(solution)/shard_map/sub | solution.py:37
  47.1 4.5 %fusion.30 = bf16[2,384,8,64]{1,3,2,0:T(8,128)(2,1)S(1)} fusion(f32[2,8,384,384]{2,3,1,0:T(8,128)} %get-tuple-element.14, f32[2,8,384]{2,1,0:T(8,128)S(1)} %get-tuple-element.13, bf16[2,384,1,8,64]{1,4,3,0,2:T(8,128)(2,1)S(1)} %copy-done), kind=kOutput, calls=%fused_computation.44 | convolution fusion | flops 307101696 | bytes 11034624 | tf_op jit(solution)/shard_map/bhqk,bkhd->bqhd/dot_general | solution.py:39
  53.8 3.8 %copy.115 = f32[1,32,2,12,1024]{4,3,2,1,0:T(8,128)} copy(f32[1,32,2,12,1024]{4,1,3,2,0:T(8,128)S(1)} %convert_bitcast_fusion.2) | data formatting | bytes 6291456 | tf_op jit(solution)/shard_map/convert_element_type | solution.py:22
  57.6 3.0 %reshape.156 = f32[768,1024]{1,0:T(8,128)S(1)} reshape(f32[1,32,2,12,1024]{4,3,2,1,0:T(8,128)} %copy.115) | data formatting | bytes 6291456 | tf_op jit(solution)/shard_map/convert_element_type | solution.py:22
  60.6 3.6 %add_convert_fusion = bf16[768,1024]{1,0:T(8,128)(2,1)} fusion(f32[768,1024]{1,0:T(8,128)S(1)} %reshape.156, bf16[768,512]{0,1:T(8,128)(2,1)} %bitcast.158, bf16[2,512,1024]{2,1,0:T(8,128)(2,1)} %param.7), kind=kOutput, calls=%fused_computation.33 | convolution fusion | flops 806879232 | bytes 6553600 | tf_op jit(solution)/shard_map/dot_general | solution.py:43
  64.3 2.5 %reshape_reshape.6 = bf16[32,2,12,1024]{3,2,1,0:T(8,128)(2,1)S(1)} reshape(bf16[768,1024]{1,0:T(8,128)(2,1)} %add_convert_fusion) | data formatting | bytes 3145728 | tf_op jit(solution)/shard_map/reshape;reshape | solution.py:62
  66.8 2.8 %copy.123 = bf16[32,12,2,1024]{3,2,1,0:T(2,128)(2,1)} copy(bf16[32,12,2,1024]{3,1,2,0:T(8,128)(2,1)S(1)} %bitcast.153) | data formatting | bytes 3145728 | tf_op jit(solution)/shard_map/transpose | solution.py:62
  69.6 3.7 %reshape.150 = bf16[8,96,1,1024]{3,1,0,2:T(8,128)(2,1)} reshape(bf16[32,12,2,1024]{3,2,1,0:T(2,128)(2,1)} %copy.123) | data formatting | bytes 3145728 | tf_op jit(solution)/shard_map/reshape | solution.py:64
  73.3 7.2 %all-to-all-start.1 = ((bf16[8,96,1,1024]{3,1,2,0:T(8,128)(2,1)}), bf16[8,96,1,1024]{3,1,2,0:T(8,128)(2,1)S(1)}, u32[]{:S(2)}, u32[]{:S(2)}) async-start(bf16[8,96,1,1024]{3,1,2,0:T(8,128)(2,1)} %bitcast.14), calls=%async_computation.1 | async-start | bytes 3145728 | tf_op jit(solution)/shard_map/all_to_all | solution.py:65
  80.7 37.2 %all-to-all-done.1 = bf16[8,96,1,1024]{3,1,2,0:T(8,128)(2,1)S(1)} async-done(((bf16[8,96,1,1024]{3,1,2,0:T(8,128)(2,1)}), bf16[8,96,1,1024]{3,1,2,0:T(8,128)(2,1)S(1)}, u32[]{:S(2)}, u32[]{:S(2)}) %all-to-all-start.1) | async-done | bytes 1572896 | tf_op jit(solution)/shard_map/all_to_all | solution.py:65
  118.9 7.4 %convolution_convert_fusion = bf16[768,1536]{1,0:T(8,128)(2,1)} fusion(bf16[2,1024,1536]{2,1,0:T(8,128)(2,1)} %param.6, f32[1024]{0:T(1024)S(1)} %bitcast.165, f32[96,8]{1,0:T(8,128)S(1)} %copy.127, bf16[8,96,1,1024]{3,1,2,0:T(8,128)(2,1)S(1)} %all-to-all-done.1), kind=kOutput, calls=%fused_computation.22 | convolution fusion | flops 2420244480 | bytes 7085056 | tf_op jit(solution)/shard_map/dot_general | solution.py:26
  126.3 6.9 %reshape.163 = bf16[2,384,3,8,64]{4,3,2,1,0:T(8,128)(2,1)} reshape(bf16[768,1536]{1,0:T(8,128)(2,1)} %convolution_convert_fusion) | data formatting | bytes 4718592 | tf_op jit(solution)/shard_map/reshape | solution.py:29
  133.2 4.3 %fusion.74 = (bf16[2,384,1,8,64]{4,3,2,1,0:T(8,128)(2,1)S(1)}, bf16[2,384,1,8,64]{4,3,2,1,0:T(8,128)(2,1)}, bf16[2,384,1,8,64]{4,3,2,1,0:T(8,128)(2,1)}) fusion(bf16[2,384,3,8,64]{4,3,2,1,0:T(8,128)(2,1)} %reshape.163), kind=kLoop, calls=%fused_computation.85 | loop fusion | bytes 4718592 | tf_op jit(solution)/shard_map/slice | solution.py:40
  137.6 2.7 %copy.147 = bf16[2,384,1,8,64]{1,4,3,0,2:T(8,128)(2,1)} copy(bf16[2,384,1,8,64]{4,3,2,1,0:T(8,128)(2,1)} %get-tuple-element.6) | data formatting | bytes 1572864
  140.3 2.7 %copy.148 = bf16[2,384,1,8,64]{1,4,3,0,2:T(8,128)(2,1)} copy(bf16[2,384,1,8,64]{4,3,2,1,0:T(8,128)(2,1)} %get-tuple-element.7) | data formatting | bytes 1572864
  143.0 1.7 copy.146
  144.7 8.2 %fusion.86 = (f32[2,8,384]{2,1,0:T(8,128)S(1)}, f32[2,8,384,384]{2,3,1,0:T(8,128)}) fusion(pred[384,384]{0,1:T(8,128)(4,1)S(1)} %broadcast_compare_fusion, bf16[2,384,1,8,64]{1,4,3,0,2:T(8,128)(2,1)} %copy.148, bf16[2,384,1,8,64]{1,4,3,0,2:T(8,128)(2,1)} %copy.147), kind=kOutput, calls=%fused_computation.89 | convolution fusion | flops 311427456 | bytes 11182080 | tf_op jit(solution)/shard_map/sub | solution.py:37
  152.9 4.5 %fusion.31 = bf16[2,384,8,64]{1,3,2,0:T(8,128)(2,1)S(1)} fusion(f32[2,8,384,384]{2,3,1,0:T(8,128)} %get-tuple-element.16, f32[2,8,384]{2,1,0:T(8,128)S(1)} %get-tuple-element.15, bf16[2,384,1,8,64]{1,4,3,0,2:T(8,128)(2,1)S(1)} %copy-done.1), kind=kOutput, calls=%fused_computation.45 | convolution fusion | flops 307101696 | bytes 11034624 | tf_op jit(solution)/shard_map/bhqk,bkhd->bqhd/dot_general | solution.py:39
  161.4 39.6 %all_to_all.33 = bf16[48,16,1024]{2,0,1:T(8,128)(2,1)S(1)} all-to-all(bf16[48,16,1024]{2,0,1:T(8,128)(2,1)S(1)} %bitcast.155), channel_id=1, replica_groups=mesh['grp'=2,'tm'=8,'space'=2] {'tm','space'}, dimensions={1} | all-to-all | bytes 3145728 | tf_op jit(solution)/shard_map/all_to_all | solution.py:73
  202.4 2.4 %reshape.155 = bf16[64,12,1024]{2,1,0:T(8,128)(2,1)S(1)} reshape(bf16[2,8,48,1024]{3,2,1,0:T(8,128)(2,1)} %bitcast.157) | data formatting | bytes 3145728 | tf_op jit(solution)/shard_map/reshape | solution.py:77
  204.8 2.0 copy.136
  (28 shorter events, 9.7 us)
Async XLA Ops:
  2.7 6.7 %copy-start.3 = (f32[2,1024]{1,0:T(2,128)S(1)}, f32[2,1024]{1,0:T(2,128)}, u32[]{:S(2)}) copy-start(f32[2,1024]{1,0:T(2,128)} %param.5) | copy-start | bytes 24580
  2.7 6.3 %all-to-all-start = ((bf16[2,32,12,1024]{3,1,2,0:T(8,128)(2,1)}), bf16[2,32,12,1024]{3,1,2,0:T(8,128)(2,1)S(1)}, u32[]{:S(2)}, u32[]{:S(2)}) async-start(bf16[2,32,12,1024]{3,1,2,0:T(8,128)(2,1)} %copy.114), calls=%async_computation | async-start | bytes 3145728 | tf_op jit(solution)/shard_map/all_to_all | solution.py:56
  38.9 8.2 %copy-start = (bf16[2,384,1,8,64]{1,4,3,0,2:T(8,128)(2,1)S(1)}, bf16[2,384,1,8,64]{1,4,3,0,2:T(8,128)(2,1)}, u32[]{:S(2)}) copy-start(bf16[2,384,1,8,64]{1,4,3,0,2:T(8,128)(2,1)} %copy.143) | copy-start | bytes 2359300
  73.3 44.6 %all-to-all-start.1 = ((bf16[8,96,1,1024]{3,1,2,0:T(8,128)(2,1)}), bf16[8,96,1,1024]{3,1,2,0:T(8,128)(2,1)S(1)}, u32[]{:S(2)}, u32[]{:S(2)}) async-start(bf16[8,96,1,1024]{3,1,2,0:T(8,128)(2,1)} %bitcast.14), calls=%async_computation.1 | async-start | bytes 3145728 | tf_op jit(solution)/shard_map/all_to_all | solution.py:65
  144.7 8.2 %copy-start.1 = (bf16[2,384,1,8,64]{1,4,3,0,2:T(8,128)(2,1)S(1)}, bf16[2,384,1,8,64]{1,4,3,0,2:T(8,128)(2,1)}, u32[]{:S(2)}) copy-start(bf16[2,384,1,8,64]{1,4,3,0,2:T(8,128)(2,1)} %copy.146) | copy-start | bytes 2359300
  157.4 1.6 copy-start.2
where the time goes:
time: 208 us; the launch traced here: 207 us
  local copies, waits for them, and re-layouts  70.2 us (34%)
  matrix products  43.7 us (21%)
  waiting for transfers between devices  39.6 us (19%)
  blocking collectives  39.6 us (19%)
  starting transfers between devices  11.1 us (5%)
  other arithmetic  2.39 us (1%)
    all_to_all x1, blocking collectives, shards(): lax.all_to_all(paired, ('tm', 'space'), split_axis=1, concat_axis=0, tile...  39.6 us
    all_to_all x1, waiting for transfers between devices, shards(): lax.all_to_all(regrouped, 'tm', split_axis=0, concat_axis=2, tiled=True)  37.2 us
    sub x2, matrix products, attend(): raised = jnp.exp(scores - row_max)  16.4 us
    unnamed x16, local copies, waits for them, and re-layouts  16 us
    reshape x2, local copies, waits for them, and re-layouts, attend(): shaped = projected.reshape(blocks, per_block, 3, HEADS, HEAD)  13.9 us
    dot_general x2, matrix products, attend(): jnp.dot(normed, qkv_weight, preferred_element_type=jnp.float32)  13.1 us
    dot_general x2, matrix products, attend(): jnp.einsum('bhqk,bkhd->bqhd', weights, shaped[:, :, 2], preferred_element...  9.06 us
    slice x2, local copies, waits for them, and re-layouts, attend(): shaped[:, :, 2]  8.7 us
  transfers between devices with their start and end apart: 2, of which 2 were waited for; matrix products, arithmetic and copies ran while one was open for 0% of the time, Pallas kernels for 0%

commit v1 on v0

--- a/solution.py
+++ b/solution.py
@@ -1,10 +1,16 @@
+import functools
+
 import jax
 import jax.numpy as jnp
 from jax import lax
+from jax.experimental import pallas as pl
+from jax.experimental.pallas import tpu as pltpu
 from jax.sharding import PartitionSpec as P
 
 HEADS = 8
 HEAD = 64
+WIDTH = 16
+MESH = pl.DeviceIdType.MESH
 
 
 def block_groups(groups, length):
@@ -78,9 +84,256 @@
     return jnp.transpose(restored, (1, 0, 2))[None]
 
 
+def head_mix(q, k, v, width):
+    rows, inner = q.shape
+    keys = k.shape[0]
+    lanes = 4 * HEAD
+    shape = (width, keys)
+    same = lax.broadcasted_iota(jnp.int32, shape, 0) == lax.rem(
+        lax.broadcasted_iota(jnp.int32, shape, 1), width
+    )
+    bias = jnp.where(same, 0.0, -1e30)[None]
+    lane = lax.broadcasted_iota(jnp.int32, (rows, lanes), 1) // HEAD
+    parts = []
+    for start in range(0, inner, lanes):
+        q4 = q[:, start : start + lanes]
+        stacked = jnp.concatenate(
+            [jnp.where(lane == i, q4, jnp.zeros_like(q4)) for i in range(4)], axis=0
+        )
+        scores = lax.dot_general(
+            stacked, k[:, start : start + lanes], (((1,), (1,)), ((), ())),
+            preferred_element_type=jnp.float32,
+        )
+        scores = scores.reshape(4 * rows // width, width, keys) + bias
+        raised = jnp.exp((scores - jnp.max(scores, axis=-1, keepdims=True)) * HEAD ** (-0.5))
+        total = jnp.sum(raised, axis=-1, keepdims=True).reshape(4 * rows, 1)
+        mixed = jnp.dot(
+            raised.reshape(4 * rows, keys).astype(jnp.bfloat16), v[:, start : start + lanes],
+            preferred_element_type=jnp.float32,
+        ) / total
+        out = mixed[:rows]
+        for i in range(1, 4):
+            out = jnp.where(lane == i, mixed[i * rows : (i + 1) * rows], out)
+        parts.append(out.astype(jnp.bfloat16))
+    return jnp.concatenate(parts, axis=1)
+
+
+def norm(x, gain):
+    wide = x.astype(jnp.float32)
+    return (
+        wide * lax.rsqrt(jnp.mean(wide * wide, axis=-1, keepdims=True) + 1e-06) * gain
+    ).astype(jnp.bfloat16)
+
+
+def dot(a, b):
+    return jnp.dot(a, b, preferred_element_type=jnp.float32)
+
+
+def kernel(
+    n, tok_hbm, gain_ref, qkv_hbm, wo_hbm, out_hbm,
+    x_vm, wqkv, wo, q_vm, kv, h_vm, h_in, mix, mix_in, out_vm,
+    x_sem, w_sem, kv_send, kv_recv, h_send, h_recv, m_send, m_recv, o_sem,
+):
+    rows, groups, width, feat = tok_hbm.shape
+    inner = wo.shape[1]
+    slots = h_in.shape[0]
+    blocks = rows * groups
+    per = rows * width
+    me = lax.axis_index("tm")
+    other = 1 - lax.axis_index("space")
+
+    def load_x(c):
+        return pltpu.make_async_copy(tok_hbm.at[:, c], x_vm.at[c], x_sem.at[c])
+
+    def load_w(i):
+        if i % 2 == 0:
+            return pltpu.make_async_copy(qkv_hbm.at[i // 2], wqkv.at[i // 2], w_sem.at[i])
+        return pltpu.make_async_copy(wo_hbm.at[i // 2], wo.at[i // 2], w_sem.at[i])
+
+    load_x(0).start()
+    load_w(0).start()
+    for c in range(1, groups):
+        load_x(c).start()
+    for i in range(1, 4):
+        load_w(i).start()
+
+    barrier = pltpu.get_barrier_semaphore()
+    pl.semaphore_signal(barrier, inc=1, device_id={"space": other}, device_id_type=MESH)
+
+    def greet(i, carry):
+        to = lax.rem(me + i, n)
+        pl.semaphore_signal(barrier, inc=1, device_id={"tm": to}, device_id_type=MESH)
+        return carry
+
+    lax.fori_loop(1, n, greet, 0)
+
+    def send_kv(c):
+        return pltpu.make_async_remote_copy(
+            src_ref=kv.at[c, 0], dst_ref=kv.at[c, 1],
+            send_sem=kv_send.at[c], recv_sem=kv_recv.at[c],
+            device_id={"space": other}, device_id_type=MESH,
+        )
+
+    def project(c):
+        load_x(c).wait()
+        normed = norm(x_vm[c].reshape(per, feat), gain_ref[0:1, :])
+        kv[c, 0] = dot(normed, wqkv[0, :, inner:]).astype(jnp.bfloat16)
+        q_vm[c] = dot(normed, wqkv[0, :, :inner]).astype(jnp.bfloat16)
+
+    load_w(0).wait()
+    project(0)
+    pl.semaphore_wait(barrier, n)
+    send_kv(0).start()
+    load_w(1).wait()
+
+    def height(c, carry):
+        @pl.when(c + 1 < groups)
+        def _():
+            project(c + 1)
+            send_kv(c + 1).start()
+
+        send_kv(c).wait()
+        both = kv[c].reshape(2 * per, 2 * inner)
+        mixture = head_mix(q_vm[c], both[:, :inner], both[:, inner:], width)
+        x = x_vm[c].reshape(per, feat).astype(jnp.float32)
+        done = (x + dot(mixture, wo[0])).astype(jnp.bfloat16)
+        h_vm[pl.ds(c * rows, rows)] = done.reshape(rows, width, feat)
+
+        def push(i, carry):
+            b = c * rows + lax.rem(i + me, rows)
+            to = lax.rem(b, n)
+            s = lax.div(b, n)
+
+            @pl.when(to == me)
+            def _():
+                pltpu.make_async_copy(h_vm.at[b], h_in.at[s, me], h_recv.at[s]).start()
+
+            @pl.when(to != me)
+            def _():
+                pltpu.make_async_remote_copy(
+                    src_ref=h_vm.at[b], dst_ref=h_in.at[s, me],
+                    send_sem=h_send, recv_sem=h_recv.at[s],
+                    device_id={"tm": to}, device_id_type=MESH,
+                ).start()
+
+            return carry
+
+        return lax.fori_loop(0, rows, push, carry)
+
+    lax.fori_loop(0, groups, height, 0)
+    load_w(2).wait()
+
+    def temporal(s, carry):
+        pltpu.make_async_copy(h_in.at[s], h_in.at[s], h_recv.at[s]).wait()
+        normed = norm(h_in[s].reshape(n * width, feat), gain_ref[1:2, :])
+        kv_now = dot(normed, wqkv[1, :, inner:]).astype(jnp.bfloat16)
+        q_now = dot(normed, wqkv[1, :, :inner]).astype(jnp.bfloat16)
+        mixture = head_mix(q_now, kv_now[:, :inner], kv_now[:, inner:], width)
+        mix[s] = mixture.reshape(n, width, inner)
+        pltpu.make_async_copy(mix.at[s, me], mix_in.at[s, me], m_recv.at[s]).start()
+
+        def push(i, carry):
+            to = lax.rem(me + i, n)
+            pltpu.make_async_remote_copy(
+                src_ref=mix.at[s, to], dst_ref=mix_in.at[s, me],
+                send_sem=m_send, recv_sem=m_recv.at[s],
+                device_id={"tm": to}, device_id_type=MESH,
+            ).start()
+            return carry
+
+        return lax.fori_loop(1, n, push, carry)
+
+    lax.fori_loop(0, slots, temporal, 0)
+    load_w(3).wait()
+
+    def finish(s, carry):
+        pltpu.make_async_copy(mix_in.at[s], mix_in.at[s], m_recv.at[s]).wait()
+        update = dot(mix_in[s].reshape(n * width, inner), wo[1])
+        h = h_vm[pl.ds(s * n, n)].reshape(n * width, feat).astype(jnp.float32)
+        out_vm[pl.ds(s * n, n)] = (h + update).astype(jnp.bfloat16).reshape(n, width, feat)
+
+        def store(i, carry):
+            b = s * n + i
+            pltpu.make_async_copy(
+                out_vm.at[b], out_hbm.at[lax.rem(b, rows), lax.div(b, rows)], o_sem
+            ).start()
+            return carry
+
+        return lax.fori_loop(0, n, store, carry)
+
+    lax.fori_loop(0, slots, finish, 0)
+    sent = slots * (n - 1)
+    pltpu.make_async_copy(h_vm.at[pl.ds(0, sent)], h_vm.at[pl.ds(0, sent)], h_send).wait()
+    pltpu.make_async_copy(
+        out_vm.at[pl.ds(0, sent), :, pl.ds(0, inner)],
+        out_vm.at[pl.ds(0, sent), :, pl.ds(0, inner)], m_send,
+    ).wait()
+    pltpu.make_async_copy(out_vm, out_vm, o_sem).wait()
+
+
+def fused(tokens, gains, qkv_weights, out_weights):
+    n = lax.axis_size("tm")
+    _, rows, cols, feat = tokens.shape
+    inner = out_weights.shape[1]
+    groups = cols // WIDTH
+    blocks = rows * groups
+    slots = blocks // n
+    per = rows * WIDTH
+    bf16 = jnp.bfloat16
+    out = pl.pallas_call(
+        functools.partial(kernel, n),
+        out_shape=jax.ShapeDtypeStruct((rows, groups, WIDTH, feat), bf16),
+        in_specs=[
+            pl.BlockSpec(memory_space=pl.ANY),
+            pl.BlockSpec(memory_space=pltpu.VMEM),
+            pl.BlockSpec(memory_space=pl.ANY),
+            pl.BlockSpec(memory_space=pl.ANY),
+        ],
+        out_specs=pl.BlockSpec(memory_space=pl.ANY),
+        scratch_shapes=[
+            pltpu.VMEM((groups, rows, WIDTH, feat), bf16),
+            pltpu.VMEM(qkv_weights.shape, bf16),
+            pltpu.VMEM(out_weights.shape, bf16),
+            pltpu.VMEM((groups, per, inner), bf16),
+            pltpu.VMEM((groups, 2, per, 2 * inner), bf16),
+            pltpu.VMEM((blocks, WIDTH, feat), bf16),
+            pltpu.VMEM((slots, n, WIDTH, feat), bf16),
+            pltpu.VMEM((slots, n, WIDTH, inner), bf16),
+            pltpu.VMEM((slots, n, WIDTH, inner), bf16),
+            pltpu.VMEM((blocks, WIDTH, feat), bf16),
+            pltpu.SemaphoreType.DMA((groups,)),
+            pltpu.SemaphoreType.DMA((4,)),
+            pltpu.SemaphoreType.DMA((groups,)),
+            pltpu.SemaphoreType.DMA((groups,)),
+            pltpu.SemaphoreType.DMA,
+            pltpu.SemaphoreType.DMA((slots,)),
+            pltpu.SemaphoreType.DMA,
+            pltpu.SemaphoreType.DMA((slots,)),
+            pltpu.SemaphoreType.DMA,
+        ],
+        compiler_params=pltpu.CompilerParams(
+            collective_id=0, has_side_effects=True, vmem_limit_bytes=50 * 2**20
+        ),
+    )(tokens.reshape(rows, groups, WIDTH, feat), gains, qkv_weights, out_weights)
+    return out.reshape(tokens.shape)
+
+
+def body(tokens, gains, qkv_weights, out_weights):
+    n = lax.axis_size("tm")
+    _, rows, cols, _ = tokens.shape
+    fits = (
+        lax.axis_size("space") == 2
+        and cols % WIDTH == 0
+        and (rows * (cols // WIDTH)) % n == 0
+        and tokens.shape[0] == 1
+    )
+    plan = fused if fits else shards
+    return plan(tokens, gains, qkv_weights, out_weights)
+
+
 def solution(mesh):
     return jax.shard_map(
-        shards,
+        body,
         mesh=mesh,
         in_specs=(P(("grp", "tm"), "space", None, None), P(), P(), P()),
         out_specs=P(("grp", "tm"), "space", None, None),

time: 208 us -> 66.6 us (0.32)
  local copies, waits for them, and re-layouts: 70.2 us -> 3.25 us
  Pallas kernels: 0 us -> 63.1 us
  matrix products: 43.7 us -> 0 us
  blocking collectives: 39.6 us -> 0 us
  waiting for transfers between devices: 39.6 us -> 0 us
  starting transfers between devices: 11.1 us -> 0 us
  other arithmetic: 2.39 us -> 0 us
    pallas_call x0 -> x1, Pallas kernels: none -> 63.1 us  [fused(): pl.pallas_call(functools.partial(kernel, n), out_shape=jax.ShapeDtypeStru...]
    all_to_all x1 -> x0, blocking collectives: 39.6 us -> none  [shards(): lax.all_to_all(paired, ('tm', 'space'), split_axis=1, concat_axis=0, tile...]
    all_to_all x2 -> x0, waiting for transfers between devices: 39.6 us -> none  [the longest x1 37.2 us: shards(): lax.all_to_all(regrouped, 'tm', split_axis=0, concat_axis=2, tiled=True)]
    dot_general x6 -> x0, matrix products: 27.3 us -> none  [the longest x2 13.1 us: attend(): jnp.dot(normed, qkv_weight, preferred_element_type=jnp.float32)]
    reshape x6 -> x0, local copies, waits for them, and re-layouts: 24 us -> none  [the longest x2 13.9 us: attend(): shaped = projected.reshape(blocks, per_block, 3, HEADS, HEAD)]
    sub x2 -> x0, matrix products: 16.4 us -> none  [attend(): raised = jnp.exp(scores - row_max)]
    convert_element_type x6 -> x0, local copies, waits for them, and re-layouts: 13.1 us -> none  [the longest x2 6.79 us: attend(): stream = tokens.astype(jnp.float32)]
    unnamed x16 -> x5, local copies, waits for them, and re-layouts: 16 us -> 3.25 us
  transfers between devices with their start and end apart: 2 -> 0, of which waited for: 2 -> 0; matrix products, arithmetic and copies ran while one was open for 0% -> 0% of each run, Pallas kernels for 0% -> 0%
where the time goes in v1:
time: 66.6 us; the launch traced here: 66.4 us
  Pallas kernels  63.1 us (95%)
  local copies, waits for them, and re-layouts  3.25 us (5%)
    pallas_call x1, Pallas kernels, fused(): pl.pallas_call(functools.partial(kernel, n), out_shape=jax.ShapeDtypeStru...  63.1 us
    unnamed x5, local copies, waits for them, and re-layouts  3.25 us

profile of v1, /device:TPU:0, one launch (start us, length us, event | category | flops | bytes accessed | tf_op | source)
XLA Modules:
  0.0 66.4 jit_solution(11835226450434387370)
XLA Ops:
  0.0 0.0 copy-start
  0.0 1.4 %copy-done = bf16[1,12,64,1024]{3,2,1,0:T(8,128)(2,1)S(1)} copy-done((bf16[1,12,64,1024]{3,2,1,0:T(8,128)(2,1)S(1)}, bf16[1,12,64,1024]{3,2,1,0:T(8,128)(2,1)}, u32[]{:S(2)}) %copy-start) | copy-done | bytes 1572888
  1.4 0.0 copy-start.1
  1.4 0.7 %copy-done.1 = f32[2,1024]{1,0:T(2,128)S(1)} copy-done((f32[2,1024]{1,0:T(2,128)S(1)}, f32[2,1024]{1,0:T(2,128)}, u32[]{:S(2)}) %copy-start.1) | copy-done | bytes 8216
  2.1 63.1 %shard_map.46 = bf16[12,4,16,1024]{3,2,1,0:T(8,128)(2,1)S(1)} custom-call(bf16[12,4,16,1024]{3,2,1,0:T(8,128)(2,1)S(1)} %bitcast.3, f32[2,1024]{1,0:T(2,128)S(1)} %copy-done.1, bf16[2,1024,1536]{2,1,0:T(8,128)(2,1)} %qkv_hbm.1, bf16[2,512,1024]{2,1,0:T(8,128)(2,1)} %wo_hbm.1), custom_call_target="tpu_custom_call" | custom-call | tf_op jit(solution)/shard_map/pallas_call | solution.py:283
  65.2 1.1 %copy.6 = bf16[1,12,64,1024]{3,2,1,0:T(8,128)(2,1)} copy(bf16[1,12,64,1024]{3,2,1,0:T(8,128)(2,1)S(1)} %bitcast.2) | data formatting | bytes 3145728
Async XLA Ops:
  0.0 1.4 %copy-start = (bf16[1,12,64,1024]{3,2,1,0:T(8,128)(2,1)S(1)}, bf16[1,12,64,1024]{3,2,1,0:T(8,128)(2,1)}, u32[]{:S(2)}) copy-start(bf16[1,12,64,1024]{3,2,1,0:T(8,128)(2,1)} %param.4) | copy-start | bytes 4718596
  1.4 0.7 %copy-start.1 = (f32[2,1024]{1,0:T(2,128)S(1)}, f32[2,1024]{1,0:T(2,128)}, u32[]{:S(2)}) copy-start(f32[2,1024]{1,0:T(2,128)} %gain_ref.1) | copy-start | bytes 24580

commit v2 on v1

--- a/solution.py
+++ b/solution.py
@@ -130,9 +130,10 @@
 
 
 def kernel(
-    n, tok_hbm, gain_ref, qkv_hbm, wo_hbm, out_hbm,
-    x_vm, wqkv, wo, q_vm, kv, h_vm, h_in, mix, mix_in, out_vm,
-    x_sem, w_sem, kv_send, kv_recv, h_send, h_recv, m_send, m_recv, o_sem,
+    n, tok_hbm, gain_hbm, qkv_hbm, wo_hbm, out_hbm,
+    gain_ref, x_vm, wqkv, wo, q_vm, kv, h_vm, h_in, mix, mix_in, out_vm,
+    gain_sem, x_sem, w_sem, kv_send, kv_recv, h_send, h_recv, m_send, m_recv, o_sem,
+    early, early_in, e_send, e_recv,
 ):
     rows, groups, width, feat = tok_hbm.shape
     inner = wo.shape[1]
@@ -150,7 +151,9 @@
             return pltpu.make_async_copy(qkv_hbm.at[i // 2], wqkv.at[i // 2], w_sem.at[i])
         return pltpu.make_async_copy(wo_hbm.at[i // 2], wo.at[i // 2], w_sem.at[i])
 
+    load_gain = pltpu.make_async_copy(gain_hbm, gain_ref, gain_sem)
     load_x(0).start()
+    load_gain.start()
     load_w(0).start()
     for c in range(1, groups):
         load_x(c).start()
@@ -174,27 +177,54 @@
             device_id={"space": other}, device_id_type=MESH,
         )
 
+    def ahead(a, b):
+        return lax.rem(lax.div(a, 2) + lax.div(b, 2), 2) == 1
+
+    def send_ahead(src, dst, send, recv, to):
+        return pltpu.make_async_remote_copy(
+            src_ref=src, dst_ref=dst, send_sem=send, recv_sem=recv,
+            device_id={"tm": to}, device_id_type=MESH,
+        )
+
     def project(c):
-        load_x(c).wait()
         normed = norm(x_vm[c].reshape(per, feat), gain_ref[0:1, :])
         kv[c, 0] = dot(normed, wqkv[0, :, inner:]).astype(jnp.bfloat16)
         q_vm[c] = dot(normed, wqkv[0, :, :inner]).astype(jnp.bfloat16)
 
+    load_x(0).wait()
+    load_gain.wait()
     load_w(0).wait()
     project(0)
     pl.semaphore_wait(barrier, n)
     send_kv(0).start()
+
+    def push_ahead(i, carry):
+        to = lax.rem(me + i, n)
+
+        @pl.when(ahead(me, to))
+        def _():
+            send_ahead(x_vm.at[0, to], h_in.at[0, me], h_send, h_recv.at[0], to).start()
+
+        return carry
+
+    lax.fori_loop(1, n, push_ahead, 0)
     load_w(1).wait()
 
     def height(c, carry):
         @pl.when(c + 1 < groups)
         def _():
+            load_x(c + 1).wait()
             project(c + 1)
             send_kv(c + 1).start()
 
         send_kv(c).wait()
         both = kv[c].reshape(2 * per, 2 * inner)
         mixture = head_mix(q_vm[c], both[:, :inner], both[:, inner:], width)
+
+        @pl.when(c == 0)
+        def _():
+            early[...] = mixture.reshape(rows, width, inner)
+
         x = x_vm[c].reshape(per, feat).astype(jnp.float32)
         done = (x + dot(mixture, wo[0])).astype(jnp.bfloat16)
         h_vm[pl.ds(c * rows, rows)] = done.reshape(rows, width, feat)
@@ -208,7 +238,13 @@
             def _():
                 pltpu.make_async_copy(h_vm.at[b], h_in.at[s, me], h_recv.at[s]).start()
 
-            @pl.when(to != me)
+            first = jnp.logical_and(s == 0, ahead(me, to))
+
+            @pl.when(first)
+            def _():
+                send_ahead(early.at[to], early_in.at[me], e_send, e_recv, to).start()
+
+            @pl.when(jnp.logical_and(to != me, jnp.logical_not(first)))
             def _():
                 pltpu.make_async_remote_copy(
                     src_ref=h_vm.at[b], dst_ref=h_in.at[s, me],
@@ -225,6 +261,17 @@
 
     def temporal(s, carry):
         pltpu.make_async_copy(h_in.at[s], h_in.at[s], h_recv.at[s]).wait()
+
+        @pl.when(s == 0)
+        def _():
+            half = early_in.at[pl.ds(0, n // 2)]
+            pltpu.make_async_copy(half, half, e_recv).wait()
+            update = dot(early_in[...].reshape(n * width, inner), wo[0])
+            frame = lax.broadcasted_iota(jnp.int32, update.shape, 0) // width
+            h = h_in[0].reshape(n * width, feat).astype(jnp.float32)
+            h = h + jnp.where(ahead(frame, me), update, 0.0)
+            h_in[0] = h.astype(jnp.bfloat16).reshape(n, width, feat)
+
         normed = norm(h_in[s].reshape(n * width, feat), gain_ref[1:2, :])
         kv_now = dot(normed, wqkv[1, :, inner:]).astype(jnp.bfloat16)
         q_now = dot(normed, wqkv[1, :, :inner]).astype(jnp.bfloat16)
@@ -268,6 +315,8 @@
         out_vm.at[pl.ds(0, sent), :, pl.ds(0, inner)],
         out_vm.at[pl.ds(0, sent), :, pl.ds(0, inner)], m_send,
     ).wait()
+    half = early.at[pl.ds(0, n // 2)]
+    pltpu.make_async_copy(half, half, e_send).wait()
     pltpu.make_async_copy(out_vm, out_vm, o_sem).wait()
 
 
@@ -284,13 +333,14 @@
         functools.partial(kernel, n),
         out_shape=jax.ShapeDtypeStruct((rows, groups, WIDTH, feat), bf16),
         in_specs=[
-            pl.BlockSpec(memory_space=pl.ANY),
-            pl.BlockSpec(memory_space=pltpu.VMEM),
-            pl.BlockSpec(memory_space=pl.ANY),
-            pl.BlockSpec(memory_space=pl.ANY),
+            pl.BlockSpec(memory_space=pltpu.HBM),
+            pl.BlockSpec(memory_space=pltpu.HBM),
+            pl.BlockSpec(memory_space=pltpu.HBM),
+            pl.BlockSpec(memory_space=pltpu.HBM),
         ],
         out_specs=pl.BlockSpec(memory_space=pl.ANY),
         scratch_shapes=[
+            pltpu.VMEM(gains.shape, jnp.float32),
             pltpu.VMEM((groups, rows, WIDTH, feat), bf16),
             pltpu.VMEM(qkv_weights.shape, bf16),
             pltpu.VMEM(out_weights.shape, bf16),
@@ -301,6 +351,7 @@
             pltpu.VMEM((slots, n, WIDTH, inner), bf16),
             pltpu.VMEM((slots, n, WIDTH, inner), bf16),
             pltpu.VMEM((blocks, WIDTH, feat), bf16),
+            pltpu.SemaphoreType.DMA,
             pltpu.SemaphoreType.DMA((groups,)),
             pltpu.SemaphoreType.DMA((4,)),
             pltpu.SemaphoreType.DMA((groups,)),
@@ -309,6 +360,10 @@
             pltpu.SemaphoreType.DMA((slots,)),
             pltpu.SemaphoreType.DMA,
             pltpu.SemaphoreType.DMA((slots,)),
+            pltpu.SemaphoreType.DMA,
+            pltpu.VMEM((rows, WIDTH, inner), bf16),
+            pltpu.VMEM((n, WIDTH, inner), bf16),
+            pltpu.SemaphoreType.DMA,
             pltpu.SemaphoreType.DMA,
         ],
         compiler_params=pltpu.CompilerParams(
@@ -326,6 +381,8 @@
         and cols % WIDTH == 0
         and (rows * (cols // WIDTH)) % n == 0
         and tokens.shape[0] == 1
+        and n % 4 == 0
+        and n <= rows
     )
     plan = fused if fits else shards
     return plan(tokens, gains, qkv_weights, out_weights)

time: 66.6 us -> 65.4 us (0.982)
  Pallas kernels: 63.1 us -> 62 us
    pallas_call x1, Pallas kernels: 63.1 us -> 62 us  [fused(): pl.pallas_call(functools.partial(kernel, n), out_shape=jax.ShapeDtypeStru...]
where the time goes in v2:
time: 65.4 us; the launch traced here: 65.2 us
  Pallas kernels  62 us (95%)
  local copies, waits for them, and re-layouts  3.25 us (5%)
    pallas_call x1, Pallas kernels, fused(): pl.pallas_call(functools.partial(kernel, n), out_shape=jax.ShapeDtypeStru...  62 us
    unnamed x5, local copies, waits for them, and re-layouts  3.25 us

profile of v2, /device:TPU:0, one launch (start us, length us, event | category | flops | bytes accessed | tf_op | source)
XLA Modules:
  0.0 65.2 jit_solution(4810133131179183260)
XLA Ops:
  0.0 0.0 copy-start
  0.0 1.4 %copy-done = bf16[1,12,64,1024]{3,2,1,0:T(8,128)(2,1)S(1)} copy-done((bf16[1,12,64,1024]{3,2,1,0:T(8,128)(2,1)S(1)}, bf16[1,12,64,1024]{3,2,1,0:T(8,128)(2,1)}, u32[]{:S(2)}) %copy-start) | copy-done | bytes 1572888
  1.4 0.0 copy-start.1
  1.4 0.7 %copy-done.1 = f32[2,1024]{1,0:T(2,128)S(1)} copy-done((f32[2,1024]{1,0:T(2,128)S(1)}, f32[2,1024]{1,0:T(2,128)}, u32[]{:S(2)}) %copy-start.1) | copy-done | bytes 8216
  2.1 62.0 %shard_map.46 = bf16[12,4,16,1024]{3,2,1,0:T(8,128)(2,1)S(1)} custom-call(bf16[12,4,16,1024]{3,2,1,0:T(8,128)(2,1)S(1)} %bitcast.3, f32[2,1024]{1,0:T(2,128)S(1)} %copy-done.1, bf16[2,1024,1536]{2,1,0:T(8,128)(2,1)} %qkv_hbm.1, bf16[2,512,1024]{2,1,0:T(8,128)(2,1)} %wo_hbm.1), custom_call_target="tpu_custom_call" | custom-call | tf_op jit(solution)/shard_map/pallas_call | solution.py:332
  64.1 1.1 %copy.6 = bf16[1,12,64,1024]{3,2,1,0:T(8,128)(2,1)} copy(bf16[1,12,64,1024]{3,2,1,0:T(8,128)(2,1)S(1)} %bitcast.2) | data formatting | bytes 3145728
Async XLA Ops:
  0.0 1.4 %copy-start = (bf16[1,12,64,1024]{3,2,1,0:T(8,128)(2,1)S(1)}, bf16[1,12,64,1024]{3,2,1,0:T(8,128)(2,1)}, u32[]{:S(2)}) copy-start(bf16[1,12,64,1024]{3,2,1,0:T(8,128)(2,1)} %param.4) | copy-start | bytes 4718596
  1.4 0.7 %copy-start.1 = (f32[2,1024]{1,0:T(2,128)S(1)}, f32[2,1024]{1,0:T(2,128)}, u32[]{:S(2)}) copy-start(f32[2,1024]{1,0:T(2,128)} %gain_hbm.1) | copy-start | bytes 24580
